TPU v7x, 32 devices: a whole 2x2x4 slice. The times are simulated.
32 devices in a mesh: parts: 2 (over x), serve: 2 (over core), tensor: 8 (over z, y).
Axes of the slice: x: 2, y: 2, z: 4, core: 2. Of those that a mesh axis runs over, the one named last changes fastest.
Arguments:
- activations: bfloat16 [2, 1536, 8192], P(None, ('parts', 'serve'), 'tensor'), parts along dimension 1, may hold values from -6 to 6
- shared_weight_matrix: bfloat16 [8192, 8192], P('tensor'), may hold values from -0.0625 to 0.0625
- adapter_down_weight: bfloat16 [16, 8192, 128], P('serve', 'tensor'), may hold values from -0.0625 to 0.0625
- adapter_up_weight: bfloat16 [16, 128, 8192], P('serve', None, 'tensor'), may hold values from -0.5 to 0.5
- adapter_rank_scale: bfloat16 [16, 128], P('serve'), may hold values from 0.5 to 2
- block_adapter_index: int32 [12], P('parts'), parts along dimension 0, may hold values from 0 to 15, as said below
Outputs:
- projected: bfloat16 [2, 1536, 8192], P(None, ('parts', 'serve'), 'tensor'), parts along dimension 1
There are 2 independent parts, one for each index of `parts`. A program takes and returns all parts, laid end to end along the dimension named above; an argument that names none is the same for every part. Nothing has to cross between parts.
Inputs may be any that keep to these rules, and one draw needn't show every extreme that they name: `block_adapter_index`: each entry names the variant of one block of 128 rows; the first two blocks name different variants.
All inputs are finite; a program needn't handle non-finite values.
Results may differ from a plain program's by a relative error of at most 0.004.
Values may be sent and summed in bfloat16 or wider, within the bound.
A program may use at most 192 MiB of HBM per device.

v0:
```python
import jax
import jax.numpy as jnp
from jax import lax
from jax.sharding import PartitionSpec as P

BLOCK = 128


def pick_rows(table, indices):
    return jnp.take(table, indices, axis=0)


def per_device(
    activations,
    shared_weight_matrix,
    adapter_down_weight,
    adapter_up_weight,
    adapter_rank_scale,
    block_adapter_index,
):
    step_count, row_count, width_dev = activations.shape
    block_count = row_count // BLOCK
    group_index = lax.axis_index("serve")
    all_down, all_up, all_scale = (
        lax.all_gather(adapter_down_weight, "serve", axis=0, tiled=True),
        lax.all_gather(adapter_up_weight, "serve", axis=0, tiled=True),
        lax.all_gather(adapter_rank_scale, "serve", axis=0, tiled=True),
    )
    served = lax.dynamic_slice_in_dim(block_adapter_index, group_index * block_count, block_count)
    selected_down_factor = pick_rows(all_down, served)
    selected_up_factor = pick_rows(all_up, served)
    selected_scale = pick_rows(all_scale, served)
    blocked = activations.reshape(step_count, block_count, BLOCK, width_dev)
    rank_part = jnp.einsum(
        "sbkd,bdr->sbkr", blocked, selected_down_factor, preferred_element_type=jnp.float32
    )
    rank_sum = lax.psum(rank_part, "tensor")
    rank_scaled = (rank_sum * selected_scale.astype(jnp.float32)[None, :, None, :]).astype(
        jnp.bfloat16
    )
    delta = jnp.einsum(
        "sbkr,brc->sbkc", rank_scaled, selected_up_factor, preferred_element_type=jnp.float32
    )
    delta = delta.reshape(step_count, row_count, delta.shape[-1])
    partial_value = jnp.einsum(
        "srd,de->sre", activations, shared_weight_matrix, preferred_element_type=jnp.float32
    )
    base = jnp.stack(
        [
            lax.psum_scatter(partial_value[step_index], "tensor", scatter_dimension=1, tiled=True)
            for step_index in range(step_count)
        ]
    )
    return (base + delta).astype(jnp.bfloat16)


def solution(mesh):
    in_specs = (
        P(None, ("parts", "serve"), "tensor"),
        P("tensor", None),
        P("serve", "tensor", None),
        P("serve", None, "tensor"),
        P("serve", None),
        P("parts"),
    )
    out_specs = P(None, ("parts", "serve"), "tensor")
    return jax.shard_map(
        per_device, mesh=mesh, in_specs=in_specs, out_specs=out_specs, check_vma=False
    )
```

profile of v0, /device:TPU:0, one launch (start us, length us, event | category | flops | bytes accessed | tf_op | source)
XLA Modules:
  0.0 550.2 jit_solution(2883599326049932335)
XLA Ops:
  6.5 0.7 all-gather.5.cloned.1.call-update
  7.3 0.0 all-gather.3.cloned.1.call-start
  7.3 0.7 all-gather.3.cloned.1.call-update
  8.0 0.0 all-reduce.2.cloned.1.call-start
  8.1 0.1 compare_and_fusion
  8.2 21.2 %fusion = f32[2,384,8192]{2,1,0:T(8,128)} fusion(bf16[2,384,1024]{2,1,0:T(8,128)(2,1)S(1)} %copy-done, bf16[1024,8192]{1,0:T(8,128)(2,1)} %param.7), kind=kOutput, calls=%fused_computation.3 | convolution fusion | flops 12884901888 | bytes 43515904 | tf_op jit(solution)/shard_map/srd,de->sre/dot_general | solution.py:45
  29.4 2.9 gather_fusion.1
  32.3 1.4 fusion.5
  33.7 0.0 all-reduce.2.cloned.1.call-update
  33.7 0.0 reduce-scatter.5.cloned.1.call-start
  33.8 19.0 %slice_bitcast_fusion.1 = (f32[384,8192]{1,0:T(8,128)}, f32[384,8192]{1,0:T(8,128)}) fusion(f32[2,384,8192]{2,1,0:T(8,128)} %fusion), kind=kLoop, calls=%fused_computation.6 | loop fusion | bytes 50331648 | tf_op jit(solution)/shard_map/squeeze | solution.py:50
  52.8 0.0 reduce-scatter.3.cloned.1.call-start
  52.8 0.5 reduce-scatter.3.cloned.1.call-update
  53.4 0.1 copy-done.2
  53.5 2.0 all_gather.11
  55.6 0.6 gather_fusion.2
  56.1 0.1 select_convert_fusion
  56.2 2.8 gather_fusion
  59.0 58.6 %all-reduce.2.cloned.1.call-done = f32[2,3,128,128]{3,2,0,1:T(8,128)} async-done(((f32[2,3,128,128]{3,2,0,1:T(8,128)}), f32[2,3,128,128]{3,2,0,1:T(8,128)}) %all-reduce.2.cloned.1.call-update) | async-done | bytes 393232 | tf_op jit(solution)/shard_map/psum | solution.py:37
  117.6 1.6 convolution_bitcast_fusion
  119.3 1.8 copy.8
  121.1 207.2 %reduce-scatter.5.cloned.1.call-done = f32[384,1024]{1,0:T(8,128)} async-done(((f32[384,8192]{1,0:T(8,128)}), f32[384,1024]{1,0:T(8,128)}) %reduce-scatter.5.cloned.1.call-update) | async-done | bytes 1572880 | tf_op jit(solution)/shard_map/reduce_scatter | solution.py:50
  328.3 210.7 %reduce-scatter.3.cloned.1.call-done = f32[384,1024]{1,0:T(8,128)} async-done(((f32[384,8192]{1,0:T(8,128)}), f32[384,1024]{1,0:T(8,128)}) %reduce-scatter.3.cloned.1.call-update) | async-done | bytes 1572880 | tf_op jit(solution)/shard_map/reduce_scatter | solution.py:50
  539.1 4.6 fusion.2
  (12 shorter events, 0.0 us)
Async XLA Ops:
  6.5 1.6 copy-start
  6.5 1.5 copy-start.3
  6.5 22.9 %all-gather.5.cloned.1.call-start = ((), (), s32[]{:S(2)}) async-start(), calls=%async_computation.5 | async-start | bytes 6291456 | tf_op jit(solution)/shard_map/all_gather | solution.py:25
  7.3 48.9 %all-gather.3.cloned.1.call-start = ((), (), s32[]{:S(2)}) async-start(), calls=%async_computation.4 | async-start | bytes 6291456 | tf_op jit(solution)/shard_map/all_gather | solution.py:26
  8.0 109.6 %all-reduce.2.cloned.1.call-start = ((), (), s32[]{:S(2)}) async-start(), calls=%async_computation.6 | async-start | bytes 786432 | tf_op jit(solution)/shard_map/psum | solution.py:37
  33.7 294.6 %reduce-scatter.5.cloned.1.call-start = ((), (), s32[]{:S(2)}) async-start(), calls=%async_computation.3 | async-start | bytes 14155776 | tf_op jit(solution)/shard_map/reduce_scatter | solution.py:50
  52.8 486.3 %reduce-scatter.3.cloned.1.call-start = ((), (), s32[]{:S(2)}) async-start(), calls=%async_computation.2 | async-start | bytes 14155776 | tf_op jit(solution)/shard_map/reduce_scatter | solution.py:50
  52.8 0.7 copy-start.2
  539.1 4.6 copy-start.1
Sparse Core Ops, SparseCore 0:
  8.9 16.3 all-gather.4
  26.9 14.8 all-gather.2
  45.1 72.5 all-reduce.1
  121.5 206.7 reduce-scatter.4
  332.2 206.7 reduce-scatter.2
where the time goes:
time: 550 us
  waiting for transfers between devices  479 us (87%)
  local copies, waits for them, and re-layouts  27.2 us (5%)
  matrix products  24.3 us (4%)
  between operations  13.2 us (2%)
    reduce_scatter x2, waiting for transfers between devices, per_device(): lax.psum_scatter(partial_value[step_index], 'tensor', scatter_dimension=1...  418 us
    psum x1, waiting for transfers between devices, per_device(): rank_sum = lax.psum(rank_part, 'tensor')  58.6 us
    dot_general x1, matrix products, per_device(): jnp.einsum('srd,de->sre', activations, shared_weight_matrix, preferred_el...  21.2 us
    squeeze x1, local copies, waits for them, and re-layouts, per_device(): partial_value[step_index]  19 us
  transfers between devices with their start and end apart: 5, of which 3 were waited for; matrix products, arithmetic and copies ran while one was open for 9% of the time, Pallas kernels for 0%

commit v1 on v0

v1 whole, which is shorter than its diff:
```python
import functools

import jax
import jax.numpy as jnp
from jax import lax
from jax.experimental import pallas as pl
from jax.experimental.pallas import tpu as pltpu
from jax.sharding import PartitionSpec as P

BLOCK = 128
TILE_ROWS = 128
MESH = pl.DeviceIdType.MESH


def chunk_at(step, place, length):
    after, before = length - 1 - place, place
    fewer = jnp.minimum(after, before)
    after_more = after > before
    interleaved = step < 2 * fewer
    count = jnp.where(interleaved, step // 2, step - fewer)
    goes_after = jnp.where(interleaved & (step % 2 == 1), jnp.logical_not(after_more), after_more)
    chunk = jnp.where(goes_after, length - 1 - count, count)
    return jnp.where(step == length - 1, place, chunk)


def base_kernel(
    length,
    x_ref,
    w_ref,
    out_ref,
    x_pair,
    w_own,
    w_pair,
    acc,
    own_sem,
    x_send,
    x_recv,
    y_send,
    y_recv,
    across_send,
    across_recv,
    core_send,
    core_recv,
    chain_send,
    chain_recv,
):
    tiles, rows, width = x_ref.shape
    part, group, index = lax.axis_index("parts"), lax.axis_index("serve"), lax.axis_index("tensor")
    side, place = index % 2, index // 2
    twin = index + 1 - 2 * side
    other_part = part + 1 - 2 * (part % 2)
    other_group = 1 - group
    quarter = width // 4
    mine = pl.multiple_of((2 * (part % 2) + group) * quarter, quarter)
    across = pl.multiple_of((2 * (other_part % 2) + group) * quarter, quarter)

    def columns(chunk, which):
        return pl.ds(pl.multiple_of((2 * chunk + which) * width, width), width)

    def own_copy(step):
        chunk = chunk_at(step, place, length)
        return pltpu.make_async_copy(
            w_ref.at[:, columns(chunk, side)], w_own.at[chunk], own_sem.at[chunk]
        )

    def x_copy(tile):
        return pltpu.make_async_remote_copy(
            src_ref=x_ref.at[tile],
            dst_ref=x_pair.at[tile],
            send_sem=x_send.at[tile],
            recv_sem=x_recv.at[tile],
            device_id={"tensor": twin},
            device_id_type=MESH,
        )

    def y_copy(step):
        chunk = chunk_at(step, place, length)
        return pltpu.make_async_remote_copy(
            src_ref=w_ref.at[pl.ds(mine, quarter), columns(chunk, 1 - side)],
            dst_ref=w_pair.at[chunk, pl.ds(mine, quarter), :],
            send_sem=y_send.at[chunk],
            recv_sem=y_recv.at[chunk],
            device_id={"tensor": twin},
            device_id_type=MESH,
        )

    def across_copy(step):
        chunk = chunk_at(step, place, length)
        block = w_pair.at[chunk, pl.ds(mine, quarter), :]
        return pltpu.make_async_remote_copy(
            src_ref=block,
            dst_ref=block,
            send_sem=across_send.at[chunk],
            recv_sem=across_recv.at[chunk],
            device_id={"parts": other_part},
            device_id_type=MESH,
        )

    def core_copy(step, which, start):
        chunk = chunk_at(step, place, length)
        block = w_pair.at[chunk, pl.ds(start, quarter), :]
        return pltpu.make_async_remote_copy(
            src_ref=block,
            dst_ref=block,
            send_sem=core_send.at[which, chunk],
            recv_sem=core_recv.at[which, chunk],
            device_id={"serve": other_group},
            device_id_type=MESH,
        )

    def chain_copy(chunk, tile, slot, target):
        return pltpu.make_async_remote_copy(
            src_ref=acc.at[chunk, tile],
            dst_ref=acc.at[slot, tile],
            send_sem=chain_send.at[chunk, tile],
            recv_sem=chain_recv.at[slot, tile],
            device_id={"tensor": target},
            device_id_type=MESH,
        )

    def forward_first(step):
        y_copy(step).wait_recv()
        across_copy(step).start()
        core_copy(step, 0, mine).start()

    def forward_second(step):
        across_copy(step).wait_recv()
        core_copy(step, 1, across).start()

    @pl.loop(0, length)
    def _(step):
        own_copy(step).start()

    barrier = pltpu.get_barrier_semaphore()
    pl.semaphore_signal(barrier, inc=1, device_id={"tensor": twin}, device_id_type=MESH)
    pl.semaphore_signal(barrier, inc=1, device_id={"parts": other_part}, device_id_type=MESH)
    pl.semaphore_signal(barrier, inc=1, device_id={"serve": other_group}, device_id_type=MESH)

    @pl.when(place > 0)
    def _():
        pl.semaphore_signal(barrier, inc=1, device_id={"tensor": index - 2}, device_id_type=MESH)

    @pl.when(place < length - 1)
    def _():
        pl.semaphore_signal(barrier, inc=1, device_id={"tensor": index + 2}, device_id_type=MESH)

    at_end = (place == 0) | (place == length - 1)
    pl.semaphore_wait(barrier, jnp.where(at_end, 4, 5))

    y_copy(0).start()

    @pl.loop(0, tiles)
    def _(tile):
        x_copy(tile).start()

    @pl.loop(1, length)
    def _(step):
        y_copy(step).start()

    forward_first(0)
    forward_second(0)

    @pl.loop(0, length)
    def _(step):
        chunk = chunk_at(step, place, length)
        own_copy(step).wait()
        core_copy(step, 0, mine).wait_recv()
        core_copy(step, 1, across).wait_recv()

        @pl.loop(0, tiles)
        def _(tile):
            @pl.when(step == 0)
            def _():
                x_copy(tile).wait_recv()

            part_sum = jnp.dot(
                x_ref[tile], w_own[chunk], preferred_element_type=jnp.float32
            ) + jnp.dot(x_pair[tile], w_pair[chunk], preferred_element_type=jnp.float32)

            @pl.when(chunk == place)
            def _():
                out_ref[tile] = part_sum

                @pl.when(place > 0)
                def _():
                    chain_copy(chunk, tile, chunk, index).wait_recv()
                    out_ref[tile] += acc[chunk, tile].astype(jnp.float32)

                @pl.when(place < length - 1)
                def _():
                    chain_copy(chunk, tile, length, index).wait_recv()
                    out_ref[tile] += acc[length, tile].astype(jnp.float32)

            @pl.when(chunk != place)
            def _():
                up = chunk > place
                first = jnp.where(up, place == 0, place == length - 1)

                @pl.when(first)
                def _():
                    acc[chunk, tile] = part_sum.astype(acc.dtype)

                @pl.when(jnp.logical_not(first))
                def _():
                    chain_copy(chunk, tile, chunk, index).wait_recv()
                    acc[chunk, tile] = (part_sum + acc[chunk, tile].astype(jnp.float32)).astype(
                        acc.dtype
                    )

                target = jnp.where(up, index + 2, index - 2)
                slot = jnp.where(chunk == place - 1, length, chunk)
                chain_copy(chunk, tile, slot, target).start()

            @pl.when((step < length - 1) & (tile == tiles // 2))
            def _():
                forward_first(step + 1)

            @pl.when((step < length - 1) & (tile == tiles - 1))
            def _():
                forward_second(step + 1)

    @pl.loop(0, tiles)
    def _(tile):
        x_copy(tile).wait_send()

    @pl.loop(0, length)
    def _(step):
        y_copy(step).wait_send()
        across_copy(step).wait_send()
        core_copy(step, 0, mine).wait_send()
        core_copy(step, 1, across).wait_send()

        chunk = chunk_at(step, place, length)

        @pl.when(chunk != place)
        def _():
            @pl.loop(0, tiles)
            def _(tile):
                chain_copy(chunk, tile, chunk, index).wait_send()


def base_sum(activations, shared_weight_matrix, length):
    row_count, width = activations.shape
    tiles = row_count // TILE_ROWS
    dma = pltpu.SemaphoreType.DMA
    return pl.pallas_call(
        functools.partial(base_kernel, length),
        out_shape=jax.ShapeDtypeStruct((tiles, TILE_ROWS, width), jnp.float32),
        in_specs=[
            pl.BlockSpec(memory_space=pltpu.VMEM),
            pl.BlockSpec(memory_space=pl.ANY),
        ],
        out_specs=pl.BlockSpec(memory_space=pltpu.VMEM),
        scratch_shapes=[
            pltpu.VMEM((tiles, TILE_ROWS, width), jnp.bfloat16),
            pltpu.VMEM((length, width, width), jnp.bfloat16),
            pltpu.VMEM((length, width, width), jnp.bfloat16),
            pltpu.VMEM((length + 1, tiles, TILE_ROWS, width), jnp.bfloat16),
            dma((length,)),
            dma((tiles,)),
            dma((tiles,)),
            dma((length,)),
            dma((length,)),
            dma((length,)),
            dma((length,)),
            dma((2, length)),
            dma((2, length)),
            dma((length, tiles)),
            dma((length + 1, tiles)),
        ],
        compiler_params=pltpu.CompilerParams(
            collective_id=0, has_side_effects=True, vmem_limit_bytes=52 * 2**20
        ),
        cost_estimate=pl.CostEstimate(
            flops=4 * row_count * width * width * length * 8,
            bytes_accessed=2 * width * width * length * 2 * 8,
            transcendentals=0,
        ),
        name="base_sum",
    )(activations.reshape(tiles, TILE_ROWS, width), shared_weight_matrix)


def pick_rows(table, served, group_index):
    held = table.shape[0]
    count = served.shape[0] // 2
    local = served - group_index * held
    here = (local >= 0) & (local < held)
    local = jnp.clip(local, 0, held - 1)
    ours = lax.dynamic_slice_in_dim(local, group_index * count, count)
    ours_here = lax.dynamic_slice_in_dim(here, group_index * count, count)
    theirs = lax.dynamic_slice_in_dim(local, (1 - group_index) * count, count)
    sent = jnp.take(table, theirs, axis=0)
    arrived = lax.ppermute(sent, "serve", [(0, 1), (1, 0)])
    kept = jnp.take(table, ours, axis=0)
    shape = (count,) + (1,) * (table.ndim - 1)
    return jnp.where(ours_here.reshape(shape), kept, arrived)


def per_device(
    length,
    activations,
    shared_weight_matrix,
    adapter_down_weight,
    adapter_up_weight,
    adapter_rank_scale,
    block_adapter_index,
):
    step_count, row_count, width_dev = activations.shape
    block_count = row_count // BLOCK
    group_index = lax.axis_index("serve")
    down = pick_rows(adapter_down_weight, block_adapter_index, group_index)
    up = pick_rows(adapter_up_weight, block_adapter_index, group_index)
    scale = pick_rows(adapter_rank_scale, block_adapter_index, group_index)
    blocked = activations.reshape(step_count, block_count, BLOCK, width_dev)
    rank_part = jnp.einsum("sbkd,bdr->sbkr", blocked, down, preferred_element_type=jnp.float32)
    rank_sum = lax.psum(rank_part, "tensor")
    base = base_sum(
        activations.reshape(step_count * row_count, width_dev), shared_weight_matrix, length
    )
    rank_scaled = (rank_sum * scale.astype(jnp.float32)[None, :, None, :]).astype(jnp.bfloat16)
    delta = jnp.einsum("sbkr,brc->sbkc", rank_scaled, up, preferred_element_type=jnp.float32)
    projected = base.reshape(delta.shape) + delta
    return projected.astype(jnp.bfloat16).reshape(activations.shape)


def solution(mesh):
    in_specs = (
        P(None, ("parts", "serve"), "tensor"),
        P("tensor", None),
        P("serve", "tensor", None),
        P("serve", None, "tensor"),
        P("serve", None),
        P("parts"),
    )
    out_specs = P(None, ("parts", "serve"), "tensor")
    return jax.shard_map(
        functools.partial(per_device, mesh.shape["tensor"] // 2),
        mesh=mesh,
        in_specs=in_specs,
        out_specs=out_specs,
        check_vma=False,
    )
```

time: 550 us -> 185 us (0.34)
  waiting for transfers between devices: 479 us -> 0.03 us
  Pallas kernels: 0 us -> 149 us
  matrix products: 24.3 us -> 6.01 us
  local copies, waits for them, and re-layouts: 27.2 us -> 10.4 us
    reduce_scatter x2 -> x0, waiting for transfers between devices: 418 us -> none  [per_device(): lax.psum_scatter(partial_value[step_index], 'tensor', scatter_dimension=1...]
    pallas_call x0 -> x1, Pallas kernels: none -> 149 us  [base_sum(): pl.pallas_call(functools.partial(base_kernel, length), out_shape=jax.Shap...]
    psum x1, waiting for transfers between devices: 58.6 us -> 0.01 us  [per_device(): rank_sum = lax.psum(rank_part, 'tensor')]
    squeeze x1 -> x0, local copies, waits for them, and re-layouts: 19 us -> none  [per_device(): partial_value[step_index]]
    dot_general x3 -> x2, matrix products: 24.3 us -> 6.01 us  [the longest x1 3.08 us: per_device(): jnp.einsum('sbkd,bdr->sbkr', blocked, down, preferred_element_type=jnp.fl...]
  transfers between devices with their start and end apart: 5 -> 4, of which waited for: 3 -> 0; matrix products, arithmetic and copies ran while one was open for 9% -> 6% of each run, Pallas kernels for 0% -> 81%
where the time goes in v1:
time: 185 us; the launch traced here: 183 us
  Pallas kernels  149 us (81%)
  between operations  13.5 us (7%)
  local copies, waits for them, and re-layouts  10.4 us (6%)
  matrix products  6.01 us (3%)
  other arithmetic  3.12 us (2%)
    pallas_call x1, Pallas kernels, base_sum(): pl.pallas_call(functools.partial(base_kernel, length), out_shape=jax.Shap...  149 us
  transfers between devices with their start and end apart: 4, of which 0 were waited for; matrix products, arithmetic and copies ran while one was open for 6% of the time, Pallas kernels for 81%

profile of v1, /device:TPU:0, one launch (start us, length us, event | category | flops | bytes accessed | tf_op | source)
XLA Modules:
  0.0 183.2 jit_solution(11417642821690188074)
XLA Ops:
  6.5 0.8 subtract_clamp_fusion
  7.4 0.1 compare_and_fusion.1
  7.4 0.7 copy-done
  8.1 0.7 gather_fusion.3
  8.9 1.0 broadcast_select_fusion
  9.9 0.5 collective-permute-start.1
  10.4 0.6 gather_fusion.5
  10.9 0.1 broadcast_select_fusion.2
  11.0 0.1 collective-permute-start.2
  11.1 2.2 %gather_fusion.1 = bf16[3,128,1024]{2,1,0:T(8,128)(2,1)S(1)} fusion(bf16[8,128,1024]{2,1,0:T(8,128)(2,1)} %param.15, s32[1024]{0:T(1024)S(1)} %pad_clamp_fusion), kind=kCustom, calls=%fused_computation.3.clone | custom fusion | bytes 1572876 | tf_op jit(solution)/shard_map/jit(_take)/gather | solution.py:292
  13.2 1.0 broadcast_select_fusion.1
  14.3 0.5 collective-permute-start
  14.7 0.1 dynamic_slice.6
  14.8 0.7 gather_fusion.2
  15.5 3.1 %fusion.3 = f32[2,3,128,128]{3,2,0,1:T(8,128)} fusion(bf16[2,3,128,1024]{3,2,1,0:T(8,128)(2,1)} %bitcast.20, bf16[3,1024,128]{2,1,0:T(8,128)(2,1)} %collective-permute-done.1, bf16[3,1024,128]{2,1,0:T(8,128)(2,1)S(1)} %gather_fusion.2, pred[3]{0:T(512)(128)(4,1)S(1)} %get-tuple-element.6, pred[3]{0:T(512)(128)(4,1)S(1)} %dynamic_slice.6), kind=kOutput, calls=%fused_computation.10 | convolution fusion | flops 202113024 | bytes 3538950 | tf_op jit(solution)/shard_map/sbkd,bdr->sbkr/dot_general | solution.py:315
  18.6 0.0 all-reduce.2.cloned.1.call-update
  18.6 0.0 copy-start.1
  18.6 1.4 copy-done.1
  20.0 149.3 %base_sum.1 = f32[6,128,1024]{2,1,0:T(8,128)} custom-call(bf16[6,128,1024]{2,1,0:T(8,128)(2,1)S(1)} %bitcast.21, bf16[1024,8192]{1,0:T(8,128)(2,1)} %w_ref.1), custom_call_target="tpu_custom_call" | custom-call | flops 103079215104 | bytes 134217728 | tf_op jit(solution)/shard_map/base_sum/pallas_call | solution.py:246
  169.3 0.6 gather_fusion.4
  169.9 2.2 %gather_fusion = bf16[3,128,1024]{2,1,0:T(8,128)(2,1)S(1)} fusion(bf16[8,128,1024]{2,1,0:T(8,128)(2,1)} %param.15, s32[1024]{0:T(1024)S(1)} %pad_clamp_fusion.1), kind=kCustom, calls=%fused_computation.clone | custom fusion | bytes 1572876 | tf_op jit(solution)/shard_map/jit(_take)/gather | solution.py:294
  172.1 0.1 fusion.15
  172.2 2.9 %fusion = bf16[2,3,128,1024]{3,2,0,1:T(8,128)(2,1)S(1)} fusion(f32[2,3,128,1024]{3,2,1,0:T(8,128)} %bitcast.22, bf16[3,128,1024]{2,1,0:T(8,128)(2,1)} %collective-permute-done, bf16[3,128,1024]{2,1,0:T(8,128)(2,1)S(1)} %gather_fusion, pred[3]{0:T(512)(128)(4,1)S(1)} %get-tuple-element.6, pred[3]{0:T(512)(128)(4,1)S(1)} %dynamic_slice.6, ...), kind=kOutput, calls=%fused_computation.7 | convolution fusion | flops 203882496 | bytes 6686214 | tf_op jit(solution)/shard_map/sbkr,brc->sbkc/dot_general | solution.py:321
  175.1 1.3 copy.9
  (13 shorter events, 0.0 us)
Async XLA Ops:
  6.5 1.6 copy-start
  6.5 3.8 %copy-start.2 = (bf16[8,128]{1,0:T(8,128)(2,1)S(1)}, bf16[8,128]{1,0:T(8,128)(2,1)}, u32[]{:S(2)}) copy-start(bf16[8,128]{1,0:T(8,128)(2,1)} %param.16) | copy-start | bytes 6148
  6.5 165.6 %all-reduce.2.cloned.1.call-start = ((), (), s32[]{:S(2)}) async-start(), calls=%async_computation | async-start | bytes 786432 | tf_op jit(solution)/shard_map/psum | solution.py:316
  8.8 5.9 %copy-start.3 = (s32[6]{0:T(128)S(1)}, s32[6]{0:T(128)}, u32[]{:S(2)}) copy-start(s32[6]{0:T(128)} %param.17) | copy-start | bytes 76
  9.9 5.6 %collective-permute-start.1 = (bf16[3,1024,128]{2,1,0:T(8,128)(2,1)}, bf16[3,1024,128]{2,1,0:T(8,128)(2,1)}, u32[]{:S(2)}, u32[]{:S(2)}) collective-permute-start(bf16[3,1024,128]{2,1,0:T(8,128)(2,1)} %broadcast_select_fusion), channel_id=1, source_target_pairs={{0,8},{8,0},{1,9},{9,1},{2,10},{10,2},{3,11},{11,3},{4,12},{12,4},... | collective-permute-start | bytes 2359304 | tf_op jit(solution)/shard_map/ppermute | solution.py:293
  11.0 161.1 %collective-permute-start.2 = (bf16[3,128]{1,0:T(4,128)(2,1)S(1)}, bf16[3,128]{1,0:T(4,128)(2,1)S(1)}, u32[]{:S(2)}, u32[]{:S(2)}) collective-permute-start(bf16[3,128]{1,0:T(4,128)(2,1)S(1)} %broadcast_select_fusion.2), channel_id=1, source_target_pairs={{0,8},{8,0},{1,9},{9,1},{2,10},{10,2},{3,11},{11,3},{4,12},{12,4},... | collective-permute-start | bytes 2312 | tf_op jit(solution)/shard_map/ppermute | solution.py:293
  14.3 157.9 %collective-permute-start = (bf16[3,128,1024]{2,1,0:T(8,128)(2,1)}, bf16[3,128,1024]{2,1,0:T(8,128)(2,1)}, u32[]{:S(2)}, u32[]{:S(2)}) collective-permute-start(bf16[3,128,1024]{2,1,0:T(8,128)(2,1)} %broadcast_select_fusion.1), channel_id=1, source_target_pairs={{0,8},{8,0},{1,9},{9,1},{2,10},{10,2},{3,11},{11,3},{4,12},{12,4},... | collective-permute-start | bytes 2359304 | tf_op jit(solution)/shard_map/ppermute | solution.py:293
  18.6 1.4 copy-start.1
Sparse Core Ops, SparseCore 0:
  18.8 75.6 all-reduce.1

commit v2 on v1

--- a/solution.py
+++ b/solution.py
@@ -8,7 +8,6 @@
 from jax.sharding import PartitionSpec as P
 
 BLOCK = 128
-TILE_ROWS = 128
 MESH = pl.DeviceIdType.MESH
 
 
@@ -23,15 +22,21 @@
     return jnp.where(step == length - 1, place, chunk)
 
 
-def base_kernel(
+def project_kernel(
     length,
     x_ref,
     w_ref,
+    rank_ref,
+    scale_ref,
+    up_ref,
     out_ref,
     x_pair,
     w_own,
     w_pair,
     acc,
+    rank_pair,
+    rank_out,
+    rank_in,
     own_sem,
     x_send,
     x_recv,
@@ -43,8 +48,11 @@
     core_recv,
     chain_send,
     chain_recv,
+    rank_send,
+    rank_recv,
 ):
     tiles, rows, width = x_ref.shape
+    blocks = up_ref.shape[0]
     part, group, index = lax.axis_index("parts"), lax.axis_index("serve"), lax.axis_index("tensor")
     side, place = index % 2, index // 2
     twin = index + 1 - 2 * side
@@ -118,6 +126,45 @@
             device_id_type=MESH,
         )
 
+    def rank_copy(which, target):
+        return pltpu.make_async_remote_copy(
+            src_ref=rank_out.at[which],
+            dst_ref=rank_in.at[which],
+            send_sem=rank_send.at[which],
+            recv_sem=rank_recv.at[which],
+            device_id={"tensor": target},
+            device_id_type=MESH,
+        )
+
+    def rank_along_chain():
+        rank_copy(0, index).wait_recv()
+        rank_pair[...] = rank_ref[...] + rank_in[0].astype(jnp.float32)
+
+        @pl.when(place == 0)
+        def _():
+            rank_in[1] = jnp.zeros_like(rank_in[1])
+
+        @pl.when(place == length - 1)
+        def _():
+            rank_in[2] = jnp.zeros_like(rank_in[2])
+
+        @pl.when(place > 0)
+        def _():
+            rank_copy(1, index).wait_recv()
+
+        @pl.when(place < length - 1)
+        def _():
+            rank_out[1] = (rank_pair[...] + rank_in[1].astype(jnp.float32)).astype(rank_out.dtype)
+            rank_copy(1, index + 2).start()
+            rank_copy(2, index).wait_recv()
+
+        @pl.when(place > 0)
+        def _():
+            rank_out[2] = (rank_pair[...] + rank_in[2].astype(jnp.float32)).astype(rank_out.dtype)
+            rank_copy(2, index - 2).start()
+
+        rank_pair[...] += rank_in[1].astype(jnp.float32) + rank_in[2].astype(jnp.float32)
+
     def forward_first(step):
         y_copy(step).wait_recv()
         across_copy(step).start()
@@ -131,6 +178,8 @@
     def _(step):
         own_copy(step).start()
 
+    rank_out[0] = rank_ref[...].astype(rank_out.dtype)
+
     barrier = pltpu.get_barrier_semaphore()
     pl.semaphore_signal(barrier, inc=1, device_id={"tensor": twin}, device_id_type=MESH)
     pl.semaphore_signal(barrier, inc=1, device_id={"parts": other_part}, device_id_type=MESH)
@@ -147,6 +196,7 @@
     at_end = (place == 0) | (place == length - 1)
     pl.semaphore_wait(barrier, jnp.where(at_end, 4, 5))
 
+    rank_copy(0, twin).start()
     y_copy(0).start()
 
     @pl.loop(0, tiles)
@@ -157,6 +207,7 @@
     def _(step):
         y_copy(step).start()
 
+    rank_along_chain()
     forward_first(0)
     forward_second(0)
 
@@ -179,17 +230,35 @@
 
             @pl.when(chunk == place)
             def _():
-                out_ref[tile] = part_sum
+                block = tile % blocks
+                scaled = (rank_pair[tile] * scale_ref[block].astype(jnp.float32)).astype(
+                    jnp.bfloat16
+                )
+                whole = part_sum + jnp.dot(
+                    scaled, up_ref[block], preferred_element_type=jnp.float32
+                )
+
+                @pl.when(place == 0)
+                def _():
+                    acc[chunk, tile] = jnp.zeros_like(acc[chunk, tile])
+
+                @pl.when(place == length - 1)
+                def _():
+                    acc[length, tile] = jnp.zeros_like(acc[length, tile])
 
                 @pl.when(place > 0)
                 def _():
                     chain_copy(chunk, tile, chunk, index).wait_recv()
-                    out_ref[tile] += acc[chunk, tile].astype(jnp.float32)
 
                 @pl.when(place < length - 1)
                 def _():
                     chain_copy(chunk, tile, length, index).wait_recv()
-                    out_ref[tile] += acc[length, tile].astype(jnp.float32)
+
+                out_ref[tile] = (
+                    whole
+                    + acc[chunk, tile].astype(jnp.float32)
+                    + acc[length, tile].astype(jnp.float32)
+                ).astype(out_ref.dtype)
 
             @pl.when(chunk != place)
             def _():
@@ -211,13 +280,23 @@
                 slot = jnp.where(chunk == place - 1, length, chunk)
                 chain_copy(chunk, tile, slot, target).start()
 
-            @pl.when((step < length - 1) & (tile == tiles // 2))
+            @pl.when((step < length - 1) & (tile == jnp.where(step == 0, tiles - 1, tiles // 2)))
             def _():
                 forward_first(step + 1)
 
             @pl.when((step < length - 1) & (tile == tiles - 1))
             def _():
                 forward_second(step + 1)
+
+    rank_copy(0, index).wait_send()
+
+    @pl.when(place < length - 1)
+    def _():
+        rank_copy(1, index).wait_send()
+
+    @pl.when(place > 0)
+    def _():
+        rank_copy(2, index).wait_send()
 
     @pl.loop(0, tiles)
     def _(tile):
@@ -239,23 +318,30 @@
                 chain_copy(chunk, tile, chunk, index).wait_send()
 
 
-def base_sum(activations, shared_weight_matrix, length):
+def project(activations, shared_weight_matrix, rank_part, scale, up, length):
     row_count, width = activations.shape
-    tiles = row_count // TILE_ROWS
+    tiles = row_count // BLOCK
+    rank = rank_part.shape[-1]
     dma = pltpu.SemaphoreType.DMA
     return pl.pallas_call(
-        functools.partial(base_kernel, length),
-        out_shape=jax.ShapeDtypeStruct((tiles, TILE_ROWS, width), jnp.float32),
+        functools.partial(project_kernel, length),
+        out_shape=jax.ShapeDtypeStruct((tiles, BLOCK, width), jnp.bfloat16),
         in_specs=[
             pl.BlockSpec(memory_space=pltpu.VMEM),
             pl.BlockSpec(memory_space=pl.ANY),
+            pl.BlockSpec(memory_space=pltpu.VMEM),
+            pl.BlockSpec(memory_space=pltpu.VMEM),
+            pl.BlockSpec(memory_space=pltpu.VMEM),
         ],
         out_specs=pl.BlockSpec(memory_space=pltpu.VMEM),
         scratch_shapes=[
-            pltpu.VMEM((tiles, TILE_ROWS, width), jnp.bfloat16),
+            pltpu.VMEM((tiles, BLOCK, width), jnp.bfloat16),
             pltpu.VMEM((length, width, width), jnp.bfloat16),
             pltpu.VMEM((length, width, width), jnp.bfloat16),
-            pltpu.VMEM((length + 1, tiles, TILE_ROWS, width), jnp.bfloat16),
+            pltpu.VMEM((length + 1, tiles, BLOCK, width), jnp.bfloat16),
+            pltpu.VMEM((tiles, BLOCK, rank), jnp.float32),
+            pltpu.VMEM((3, tiles, BLOCK, rank), jnp.bfloat16),
+            pltpu.VMEM((3, tiles, BLOCK, rank), jnp.bfloat16),
             dma((length,)),
             dma((tiles,)),
             dma((tiles,)),
@@ -267,6 +353,8 @@
             dma((2, length)),
             dma((length, tiles)),
             dma((length + 1, tiles)),
+            dma((3,)),
+            dma((3,)),
         ],
         compiler_params=pltpu.CompilerParams(
             collective_id=0, has_side_effects=True, vmem_limit_bytes=52 * 2**20
@@ -276,8 +364,14 @@
             bytes_accessed=2 * width * width * length * 2 * 8,
             transcendentals=0,
         ),
-        name="base_sum",
-    )(activations.reshape(tiles, TILE_ROWS, width), shared_weight_matrix)
+        name="project",
+    )(
+        activations.reshape(tiles, BLOCK, width),
+        shared_weight_matrix,
+        rank_part.reshape(tiles, BLOCK, rank),
+        scale[:, None, :],
+        up,
+    )
 
 
 def pick_rows(table, served, group_index):
@@ -313,14 +407,15 @@
     scale = pick_rows(adapter_rank_scale, block_adapter_index, group_index)
     blocked = activations.reshape(step_count, block_count, BLOCK, width_dev)
     rank_part = jnp.einsum("sbkd,bdr->sbkr", blocked, down, preferred_element_type=jnp.float32)
-    rank_sum = lax.psum(rank_part, "tensor")
-    base = base_sum(
-        activations.reshape(step_count * row_count, width_dev), shared_weight_matrix, length
+    projected = project(
+        activations.reshape(step_count * row_count, width_dev),
+        shared_weight_matrix,
+        rank_part,
+        scale,
+        up,
+        length,
     )
-    rank_scaled = (rank_sum * scale.astype(jnp.float32)[None, :, None, :]).astype(jnp.bfloat16)
-    delta = jnp.einsum("sbkr,brc->sbkc", rank_scaled, up, preferred_element_type=jnp.float32)
-    projected = base.reshape(delta.shape) + delta
-    return projected.astype(jnp.bfloat16).reshape(activations.shape)
+    return projected.reshape(activations.shape)
 
 
 def solution(mesh):

time: 185 us -> 175 us (0.946)
  between operations: 13.5 us -> 0.09 us
  Pallas kernels: 149 us -> 153 us
  matrix products: 6.01 us -> 3.45 us
    pallas_call x1, Pallas kernels: 149 us -> 153 us  [project(): pl.pallas_call(functools.partial(project_kernel, length), out_shape=jax.S...]
    dot_general x1 -> x0, matrix products: 2.92 us -> none  [per_device(): jnp.einsum('sbkr,brc->sbkc', rank_scaled, up, preferred_element_type=jnp....]
  transfers between devices with their start and end apart: 4 -> 3, of which waited for: 0 -> 0; matrix products, arithmetic and copies ran while one was open for 6% -> 7% of each run, Pallas kernels for 81% -> 0%
where the time goes in v2:
time: 175 us; the launch traced here: 174 us
  Pallas kernels  153 us (87%)
  local copies, waits for them, and re-layouts  11.7 us (7%)
  other arithmetic  4.4 us (3%)
  matrix products  3.45 us (2%)
    pallas_call x1, Pallas kernels, project(): pl.pallas_call(functools.partial(project_kernel, length), out_shape=jax.S...  153 us
    gather x3, local copies, waits for them, and re-layouts, pick_rows(): kept = jnp.take(table, ours, axis=0)  4.31 us
  transfers between devices with their start and end apart: 3, of which 0 were waited for; matrix products, arithmetic and copies ran while one was open for 7% of the time, Pallas kernels for 0%

profile of v2, /device:TPU:0, one launch (start us, length us, event | category | flops | bytes accessed | tf_op | source)
XLA Modules:
  0.0 174.1 jit_solution(11060358726413926739)
XLA Ops:
  0.0 0.8 subtract_clamp_fusion
  0.8 0.1 compare_and_fusion.1
  0.9 2.3 %gather_fusion.1 = bf16[3,1024,128]{2,1,0:T(8,128)(2,1)S(1)} fusion(bf16[8,1024,128]{2,1,0:T(8,128)(2,1)} %param.14, s32[1024]{0:T(1024)S(1)} %pad_clamp_fusion), kind=kCustom, calls=%fused_computation.3.clone | custom fusion | bytes 1572876 | tf_op jit(solution)/shard_map/jit(_take)/gather | solution.py:386
  3.2 0.0 copy-start.1
  3.2 0.0 copy-start.2
  3.2 1.0 broadcast_select_fusion.1
  4.2 0.5 collective-permute-start
  4.7 0.6 gather_fusion.5
  5.3 1.0 broadcast_select_fusion
  6.3 0.1 collective-permute-start.2
  6.4 0.6 gather_fusion.3
  7.0 0.1 broadcast_select_fusion.2
  7.0 0.5 collective-permute-start.1
  7.5 0.6 gather_fusion.4
  8.1 3.2 %gather_fusion = bf16[3,1024,128]{2,1,0:T(8,128)(2,1)} fusion(bf16[8,1024,128]{2,1,0:T(8,128)(2,1)} %param.14, s32[1024]{0:T(1024)S(1)} %pad_clamp_fusion.1), kind=kCustom, calls=%fused_computation.clone | custom fusion | bytes 1572876 | tf_op jit(solution)/shard_map/jit(_take)/gather | solution.py:388
  11.3 0.6 gather_fusion.2
  11.8 0.1 dynamic_slice.6
  11.9 0.1 fusion.9
  12.0 0.0 collective-permute-done
  12.0 3.4 %fusion.2 = f32[2,3,128,128]{2,3,0,1:T(8,128)} fusion(bf16[2,3,128,1024]{3,2,1,0:T(8,128)(2,1)} %bitcast.15, bf16[3,1024,128]{2,1,0:T(8,128)(2,1)} %collective-permute-done, bf16[3,1024,128]{2,1,0:T(8,128)(2,1)} %gather_fusion, pred[3]{0:T(512)(128)(4,1)S(1)} %get-tuple-element.6, pred[3]{0:T(512)(128)(4,1)S(1)} %dynamic_slice.6), kind=kOutput, calls=%fused_computation.8 | convolution fusion | flops 202113024 | bytes 3538950 | tf_op jit(solution)/shard_map/sbkd,bdr->sbkr/dot_general | solution.py:409
  15.5 1.2 copy.12
  16.6 1.3 select_select_fusion.up_ref
  17.9 153.5 %project.1 = bf16[6,128,1024]{2,1,0:T(8,128)(2,1)} custom-call(bf16[6,128,1024]{2,1,0:T(8,128)(2,1)} %bitcast.16, bf16[1024,8192]{1,0:T(8,128)(2,1)} %w_ref.1, f32[6,128,128]{2,1,0:T(8,128)S(1)} %bitcast.13, bf16[3,1,128]{2,1,0:T(2,128)(2,1)S(1)} %copy.13.scale_ref, bf16[3,128,1024]{2,1,0:T(8,128)(2,1)S(1)} %select_select_fusion.up_ref), custom_call_target="tpu_custom_call" | custom-call | flops 103079215104 | bytes 134217728 | tf_op jit(solution)/shard_map/project/pallas_call | solution.py:326
  171.4 2.7 %copy.22 = bf16[2,384,1024]{2,1,0:T(8,128)(2,1)} copy(bf16[2,384,1024]{2,1,0:T(8,128)(2,1)} %bitcast.14) | data formatting | bytes 3145728
  (10 shorter events, 0.0 us)
Async XLA Ops:
  0.0 4.7 %copy-start = (bf16[8,128,1024]{2,1,0:T(8,128)(2,1)S(1)}, bf16[8,128,1024]{2,1,0:T(8,128)(2,1)}, u32[]{:S(2)}) copy-start(bf16[8,128,1024]{2,1,0:T(8,128)(2,1)} %param.15) | copy-start | bytes 6291460
  3.2 3.2 %copy-start.1 = (bf16[8,128]{1,0:T(8,128)(2,1)S(1)}, bf16[8,128]{1,0:T(8,128)(2,1)}, u32[]{:S(2)}) copy-start(bf16[8,128]{1,0:T(8,128)(2,1)} %param.16) | copy-start | bytes 6148
  3.2 4.3 %copy-start.2 = (s32[6]{0:T(128)S(1)}, s32[6]{0:T(128)}, u32[]{:S(2)}) copy-start(s32[6]{0:T(128)} %param.17) | copy-start | bytes 76
  4.2 7.8 %collective-permute-start = (bf16[3,1024,128]{2,1,0:T(8,128)(2,1)}, bf16[3,1024,128]{2,1,0:T(8,128)(2,1)}, u32[]{:S(2)}, u32[]{:S(2)}) collective-permute-start(bf16[3,1024,128]{2,1,0:T(8,128)(2,1)} %broadcast_select_fusion.1), channel_id=1, source_target_pairs={{0,8},{8,0},{1,9},{9,1},{2,10},{10,2},{3,11},{11,3},{4,12},{12,4},... | collective-permute-start | bytes 2359304 | tf_op jit(solution)/shard_map/ppermute | solution.py:387
  6.3 10.3 %collective-permute-start.2 = (bf16[3,128,1024]{2,1,0:T(8,128)(2,1)}, bf16[3,128,1024]{2,1,0:T(8,128)(2,1)}, u32[]{:S(2)}, u32[]{:S(2)}) collective-permute-start(bf16[3,128,1024]{2,1,0:T(8,128)(2,1)} %broadcast_select_fusion), channel_id=1, source_target_pairs={{0,8},{8,0},{1,9},{9,1},{2,10},{10,2},{3,11},{11,3},{4,12},{12,4},... | collective-permute-start | bytes 2359304 | tf_op jit(solution)/shard_map/ppermute | solution.py:387
  7.0 4.9 %collective-permute-start.1 = (bf16[3,128]{1,0:T(4,128)(2,1)S(1)}, bf16[3,128]{1,0:T(4,128)(2,1)S(1)}, u32[]{:S(2)}, u32[]{:S(2)}) collective-permute-start(bf16[3,128]{1,0:T(4,128)(2,1)S(1)} %broadcast_select_fusion.2), channel_id=1, source_target_pairs={{0,8},{8,0},{1,9},{9,1},{2,10},{10,2},{3,11},{11,3},{4,12},{12,4},... | collective-permute-start | bytes 2312 | tf_op jit(solution)/shard_map/ppermute | solution.py:387
